TPU v7x, 32 devices: a whole 2x2x4 slice. The times are simulated.
32 devices in a mesh: imp: 4 (over x, core), dev: 8 (over z, y).
Axes of the slice: x: 2, y: 2, z: 4, core: 2. Of those that a mesh axis runs over, the one named last changes fastest.
Arguments:
- values: bfloat16 [2048, 256, 256], P(('imp', 'dev')), may hold values from 0 to 1
- costs: bfloat16 [2048, 256, 256], P(('imp', 'dev')), may hold values from 0.19921875 to 2
- block_ids: int32 [2048], P(('imp', 'dev')), may hold values from 0 to 31
- row_counts: int32 [2048], P(('imp', 'dev')), may hold values from 32 to 256
- adv_map: int32 [8192], P(('imp', 'dev')), may hold values from 0 to 2047
- camp_limits: float32 [8192], P(('imp', 'dev')), may hold values from 2048 to 16384
- adv_limits: float32 [2048], replicated, may hold values from 8192 to 32768
- camp_duals: float32 [8192], P(('imp', 'dev')), may hold values from 0 to 0.5
- adv_duals: float32 [2048], replicated, may hold values from 0 to 0.2
Outputs:
- camp_final: float32 [8192], P(('imp', 'dev'))
- adv_final: float32 [2048], replicated
- spend: float32 [8192], P(('imp', 'dev'))
All inputs are finite; a program needn't handle non-finite values.
Results may differ from a plain program's by a relative error of at most 0.0003.
Values sent between devices are 32-bit elements; how exact they have to be, the bound alone decides.
A program may use at most 64 MiB of HBM per device.

v0:
```python
import jax
import jax.numpy as jnp
from jax import lax
from jax.sharding import PartitionSpec as P

ITERS = 2


def local_partial(values, costs, onehot, live, price_all):
    price_blocks = jnp.dot(onehot, price_all, precision=lax.Precision.HIGHEST)
    cost_f = costs.astype(jnp.float32)
    x_val = (
        jnp.clip((values.astype(jnp.float32) - cost_f * price_blocks[:, None, :]) / 0.5, 0.0, 1.0)
        * live
    )
    contrib = jnp.sum(cost_f * x_val, axis=1)
    return jnp.dot(onehot.T, contrib, precision=lax.Precision.HIGHEST).reshape(-1)


def body(
    values, costs, block_ids, row_counts, adv_map, camp_limits, adv_limits, camp_duals, adv_duals
):
    owned = camp_duals.shape[0]
    devices = lax.axis_size(("imp", "dev"))
    total = owned * devices
    blocks_here = values.shape[0]
    rows = values.shape[1]
    width = values.shape[2]
    num_blocks = total // width
    num_adv = adv_duals.shape[0]
    eta = owned // width / (4.0 * rows * blocks_here)
    eta_adv = num_adv * (owned // width) / (4.0 * rows * blocks_here * total)
    onehot = (block_ids[:, None] == jnp.arange(num_blocks, dtype=jnp.int32)[None, :]).astype(
        jnp.float32
    )
    row_index = jnp.arange(rows, dtype=jnp.int32)
    live = (row_index[None, :] < row_counts[:, None]).astype(jnp.float32)[:, :, None]
    mu = adv_duals
    lam = camp_duals
    spend = jnp.zeros((owned,), jnp.float32)
    for step in range(ITERS):
        price_own = lam + mu[adv_map]
        price_all = lax.all_gather(price_own, ("imp", "dev"), axis=0, tiled=True).reshape(
            num_blocks, width
        )
        partial_value = local_partial(values, costs, onehot, live, price_all)
        summed = lax.psum(partial_value, ("imp", "dev"))
        spend = lax.dynamic_slice_in_dim(summed, lax.axis_index(("imp", "dev")) * owned, owned, 0)
        adv_part = jax.ops.segment_sum(spend, adv_map, num_adv)
        adv_spend = lax.psum(adv_part, ("imp", "dev"))
        lam = jnp.maximum(0.0, lam + eta * (spend - camp_limits))
        mu = jnp.maximum(0.0, mu + eta_adv * (adv_spend - adv_limits))
    return (lam, mu, spend)


def solution(mesh):
    placed = (
        P(("imp", "dev"), None, None),
        P(("imp", "dev"), None, None),
        P(("imp", "dev")),
        P(("imp", "dev")),
        P(("imp", "dev")),
        P(("imp", "dev")),
        P(),
        P(("imp", "dev")),
        P(),
    )
    return jax.shard_map(
        body,
        mesh=mesh,
        in_specs=placed,
        out_specs=(P(("imp", "dev")), P(), P(("imp", "dev"))),
        check_vma=False,
    )
```

profile of v0, /device:TPU:0, one launch (start us, length us, event | category | flops | bytes accessed | tf_op | source)
XLA Modules:
  0.0 325.4 jit_solution(1436974897066493996)
XLA Ops:
  0.6 0.7 compare_select_fusion
  1.3 1.9 gather_fusion
  3.3 0.7 add.43
  3.9 69.7 %all-gather = f32[32,1,256]{2,1,0:T(1,128)S(1)} all-gather(f32[1,1,256]{2,1,0:T(1,128)S(1)} %bitcast.18), channel_id=1, replica_groups=mesh['imp'=4,'dev'=8] {'imp','dev'}, dimensions={0}, use_global_device_ids=true | all-gather | bytes 33792 | tf_op jit(solution)/shard_map/all_gather | solution.py:43
  73.7 0.9 fusion.12
  74.6 0.7 fusion.8
  75.3 0.0 copy-start.2
  75.3 9.1 %fusion.6 = f32[64,256]{1,0:T(8,128)S(1)} fusion(bf16[64,256,256]{2,1,0:T(8,128)(2,1)} %param.9, bf16[64,256,256]{2,1,0:T(8,128)(2,1)} %param.10, f32[64,256]{1,0:T(8,128)S(1)} %fusion.8, f32[64,256]{1,0:T(8,128)S(1)} %fusion.12), kind=kLoop, calls=%fused_computation.16 | loop fusion | flops 37732352 | bytes 16973824 | tf_op jit(solution)/shard_map/reduce_sum | solution.py:16
  84.5 0.3 convolution_bitcast_fusion.1
  84.8 37.0 %psum.28 = f32[8192]{0:T(1024)S(1)} all-reduce(f32[8192]{0:T(1024)S(1)} %bitcast.16), channel_id=1, replica_groups=mesh['imp'=4,'dev'=8] {'imp','dev'}, use_global_device_ids=true, to_apply=%region_1.2 | all-reduce | flops 8192 | bytes 65536 | tf_op jit(solution)/shard_map/psum | solution.py:47
  121.8 0.1 dynamic_slice.6
  121.9 2.1 scatter_custom_fusion
  124.0 41.4 %psum.29 = f32[2048]{0:T(1024)S(1)} all-reduce(f32[2048]{0:T(1024)S(1)} %scatter_custom_fusion), channel_id=1, replica_groups=mesh['imp'=4,'dev'=8] {'imp','dev'}, use_global_device_ids=true, to_apply=%region_3.4 | all-reduce | flops 2048 | bytes 16384 | tf_op jit(solution)/shard_map/psum | solution.py:50
  165.5 1.7 gather_fusion.1
  167.2 0.1 fusion.23
  167.3 65.7 %all-gather.1 = f32[32,1,256]{2,1,0:T(1,128)S(1)} all-gather(f32[1,1,256]{2,1,0:T(1,128)S(1)} %bitcast.19), channel_id=1, replica_groups=mesh['imp'=4,'dev'=8] {'imp','dev'}, dimensions={0}, use_global_device_ids=true | all-gather | bytes 33792 | tf_op jit(solution)/shard_map/all_gather | solution.py:43
  232.9 0.2 fusion.9
  233.2 9.1 %fusion.7 = f32[64,256]{1,0:T(8,128)S(1)} fusion(bf16[64,256,256]{2,1,0:T(8,128)(2,1)} %param.9, bf16[64,256,256]{2,1,0:T(8,128)(2,1)} %param.10, f32[64,256]{1,0:T(8,128)S(1)} %fusion.9, f32[64,256]{1,0:T(8,128)S(1)} %fusion.8), kind=kLoop, calls=%fused_computation.17 | loop fusion | flops 37732352 | bytes 16973824 | tf_op jit(solution)/shard_map/reduce_sum | solution.py:16
  242.3 0.3 convolution_bitcast_fusion
  242.6 37.3 %psum.30 = f32[8192]{0:T(1024)S(1)} all-reduce(f32[8192]{0:T(1024)S(1)} %bitcast.17), channel_id=1, replica_groups=mesh['imp'=4,'dev'=8] {'imp','dev'}, use_global_device_ids=true, to_apply=%region_5.6 | all-reduce | flops 8192 | bytes 65536 | tf_op jit(solution)/shard_map/psum | solution.py:47
  279.9 0.6 add_maximum_fusion.2
  280.5 2.1 scatter_custom_fusion.1
  282.6 42.2 %psum.31 = f32[2048]{0:T(1024)S(1)} all-reduce(f32[2048]{0:T(1024)S(1)} %scatter_custom_fusion.1), channel_id=1, replica_groups=mesh['imp'=4,'dev'=8] {'imp','dev'}, use_global_device_ids=true, to_apply=%region_7.8 | all-reduce | flops 2048 | bytes 16384 | tf_op jit(solution)/shard_map/psum | solution.py:50
  324.8 0.6 add_maximum_fusion
  (15 shorter events, 0.1 us)
Async XLA Ops:
  75.3 9.2 %copy-start.3 = (s32[64]{0:T(128)S(1)}, s32[64]{0:T(128)}, u32[]{:S(2)}) copy-start(s32[64]{0:T(128)} %param.11) | copy-start | bytes 772
  75.3 90.1 %copy-start = (f32[2048]{0:T(1024)S(1)}, f32[2048]{0:T(1024)}, u32[]{:S(2)}) copy-start(f32[2048]{0:T(1024)} %param.17) | copy-start | bytes 24580
  75.3 90.1 %copy-start.1 = (f32[2048]{0:T(1024)S(1)}, f32[2048]{0:T(1024)}, u32[]{:S(2)}) copy-start(f32[2048]{0:T(1024)} %param.15) | copy-start | bytes 24580
  75.3 91.9 %copy-start.2 = (f32[256]{0:T(256)S(1)}, f32[256]{0:T(256)}, u32[]{:S(2)}) copy-start(f32[256]{0:T(256)} %param.16) | copy-start | bytes 3076
  75.3 91.9 %copy-start.4 = (f32[256]{0:T(256)S(1)}, f32[256]{0:T(256)}, u32[]{:S(2)}) copy-start(f32[256]{0:T(256)} %param.14) | copy-start | bytes 3076
  280.5 44.9 %copy-start.5 = (f32[256]{0:T(256)}, f32[256]{0:T(256)S(1)}, u32[]{:S(2)}) copy-start(f32[256]{0:T(256)S(1)} %get-tuple-element.4) | copy-start | bytes 3076
where the time goes:
time: 326 us; the launch traced here: 325 us
  blocking collectives  293 us (90%)
  other arithmetic  25.8 us (8%)
  local copies, waits for them, and re-layouts  3.81 us (1%)
    all_gather x2, blocking collectives, body(): lax.all_gather(price_own, ('imp', 'dev'), axis=0, tiled=True)  135 us
    psum x2, blocking collectives, body(): adv_spend = lax.psum(adv_part, ('imp', 'dev'))  83.6 us
    psum x2, blocking collectives, body(): summed = lax.psum(partial_value, ('imp', 'dev'))  74.3 us
    reduce_sum x2, other arithmetic, local_partial(): contrib = jnp.sum(cost_f * x_val, axis=1)  18.2 us

commit v1 on v0

v1 whole, which is shorter than its diff:
```python
import functools

import jax
import jax.numpy as jnp
from jax import lax
from jax.experimental import pallas as pl
from jax.experimental.pallas import tpu as pltpu
from jax.sharding import PartitionSpec as P

ITERS = 2
LANES = 128
SLAB = 16
SUBLANES = 8
CHUNKS = 8
MESH = pl.DeviceIdType.MESH


def split3(x):
    one = x.astype(jnp.bfloat16)
    rest = x - one.astype(jnp.float32)
    two = rest.astype(jnp.bfloat16)
    three = (rest - two.astype(jnp.float32)).astype(jnp.bfloat16)
    return jnp.concatenate([one, two, three], axis=0)


def sum3(x):
    m = x.shape[0] // 3
    return x[:m] + x[m : 2 * m] + x[2 * m :]


def low_onehot(adv):
    width = adv.shape[1]
    rows = lax.broadcasted_iota(jnp.int32, (LANES, width), 0)
    hit = rows == jnp.bitwise_and(adv, LANES - 1)
    return jnp.where(hit, 1.0, 0.0).astype(jnp.bfloat16)


def high_onehot(adv, groups):
    width = adv.shape[1]
    rows = lax.broadcasted_iota(jnp.int32, (groups, width), 0)
    return jnp.where(rows == lax.shift_right_logical(adv, 7), 1.0, 0.0)


def take(mu3, low, high):
    picked = jnp.dot(mu3, low, preferred_element_type=jnp.float32)
    return jnp.sum(sum3(picked) * high, axis=0, keepdims=True)


def kernel(
    n,
    n_dev,
    eta,
    eta_adv,
    counts_s,
    values,
    costs,
    ids_v,
    adv_ref,
    lim_ref,
    adv_lim_ref,
    lam_ref,
    mu_ref,
    lam_out,
    mu_out,
    spend_out,
    vbuf,
    cbuf,
    price,
    static,
    low,
    high,
    cap,
    contrib,
    asked,
    part,
    got,
    allspend,
    load_sem,
    send_sem,
    recv_sem,
):
    blocks, rows, width = vbuf.shape
    groups = mu_ref.shape[0]
    me = lax.axis_index("imp") * n_dev + lax.axis_index("dev")
    step_blocks = blocks // CHUNKS

    def load(i):
        where = pl.ds(i * step_blocks, step_blocks)
        return (
            pltpu.make_async_copy(values.at[where], vbuf.at[where], load_sem.at[0, i]),
            pltpu.make_async_copy(costs.at[where], cbuf.at[where], load_sem.at[1, i]),
        )

    for i in range(CHUNKS):
        for copy in load(i):
            copy.start()

    barrier = pltpu.get_barrier_semaphore()

    def peer(d):
        return lax.rem(me + d, n)

    def place(k):
        return (k // n_dev, lax.rem(k, n_dev))

    @pl.loop(1, n)
    def _(d):
        pl.semaphore_signal(barrier, inc=1, device_id=place(peer(d)), device_id_type=MESH)

    def lanes(k):
        return pl.ds(pl.multiple_of(k * width, width), width)

    def share(ref, phase):
        @pl.loop(1, n)
        def _(d):
            spot = ref.at[:, lanes(me)]
            pltpu.make_async_remote_copy(
                src_ref=spot,
                dst_ref=spot,
                send_sem=send_sem.at[phase],
                recv_sem=recv_sem.at[phase],
                device_id=place(peer(d)),
                device_id_type=MESH,
            ).start()

    def wait_all(ref, sem):
        span = ref.at[:, pl.ds(0, (n - 1) * width)]
        pltpu.make_async_copy(span, span, sem).wait()

    def scatter(phase):
        @pl.loop(1, n)
        def _(d):
            to = peer(d)
            pltpu.make_async_remote_copy(
                src_ref=part.at[to],
                dst_ref=got.at[phase, d - 1],
                send_sem=send_sem.at[2 + phase],
                recv_sem=recv_sem.at[2 + phase],
                device_id=place(to),
                device_id_type=MESH,
            ).start()

    def wait_scatter(sem, phase):
        span = got.at[phase]
        pltpu.make_async_copy(span, span, sem).wait()

    adv = adv_ref[...]
    lam = lam_ref[...]
    mu = mu_ref[...]
    price[0, :, lanes(me)] = lam + take(split3(mu), low_onehot(adv), high_onehot(adv, groups))
    static[:, lanes(me)] = jnp.concatenate(
        [lam, adv.astype(jnp.float32), lim_ref[...], jnp.zeros_like(lam)], axis=0
    )
    live_rows = lax.broadcasted_iota(jnp.int32, (SLAB, LANES), 0)
    for k in range(SLAB + 1):
        cap[k] = jnp.where(live_rows < k, 0.5, 0.0)

    pl.semaphore_wait(barrier, n - 1)
    share(price.at[0], 0)
    share(static, 1)
    wait_all(price.at[0], recv_sem.at[0])

    campaign = lax.broadcasted_iota(jnp.int32, (part.shape[0], blocks), 0)
    owner = jnp.where(campaign == ids_v[...], 1.0, 0.0).astype(jnp.bfloat16)
    asks3 = jnp.concatenate([owner, owner, owner], axis=0)
    wide = lax.broadcasted_iota(jnp.int32, (blocks, blocks * SUBLANES), 1)
    from_block = lax.broadcasted_iota(jnp.int32, (blocks, blocks * SUBLANES), 0)
    spread = jnp.where(lax.shift_right_logical(wide, 3) == from_block, 1.0, 0.0)
    owner = jnp.dot(
        owner, spread.astype(jnp.bfloat16), preferred_element_type=jnp.float32
    ).astype(jnp.bfloat16)
    owner3 = jnp.concatenate([owner, owner, owner], axis=1)

    def block_pass(b, it):
        prices = [
            jnp.broadcast_to(asked[b, :, h : h + LANES], (SLAB, LANES))
            for h in range(0, width, LANES)
        ]
        totals = [jnp.zeros((SLAB, LANES), jnp.float32) for _ in prices]
        count = counts_s[b]
        for s in range(0, rows, SLAB):
            top = cap[jnp.minimum(jnp.maximum(count - s, 0), SLAB)]
            for h, p in enumerate(prices):
                at = pl.ds(h * LANES, LANES)
                v = vbuf[b, pl.ds(s, SLAB), at].astype(jnp.float32)
                c = cbuf[b, pl.ds(s, SLAB), at].astype(jnp.float32)
                x = jnp.minimum(jnp.maximum(v - c * p, 0.0), top)
                totals[h] = totals[h] + c * x
        for h, total in enumerate(totals):
            where = pl.ds(pl.multiple_of(b * SUBLANES, SUBLANES), SUBLANES)
            contrib[where, pl.ds(h * LANES, LANES)] = 2.0 * (
                total[:SUBLANES] + total[SUBLANES:]
            )

    for it in range(ITERS):
        offers = jnp.concatenate(
            [price[it, :, pl.ds(k * width, width)] for k in range(part.shape[0])], axis=0
        )
        asking = lax.dot_general(
            asks3, split3(offers), (((0,), (0,)), ((), ())), preferred_element_type=jnp.float32
        )
        for b in range(blocks):
            asked[b] = asking[b : b + 1]
        for i in range(CHUNKS if it == 0 else 1):
            if it == 0:
                for copy in load(i):
                    copy.wait()
            span = step_blocks if it == 0 else blocks

            @pl.loop(i * span, (i + 1) * span)
            def _(b):
                block_pass(b, it)

        mine = jnp.dot(owner3, split3(contrib[...]), preferred_element_type=jnp.float32)
        if it > 0:
            wait_scatter(send_sem.at[2 + it - 1], it - 1)
        for k in range(part.shape[0]):
            part[k] = mine[k : k + 1]
        scatter(it)
        if it == 0:
            wait_all(static, recv_sem.at[1])
            for k in range(n):
                every = static[1:2, pl.ds(k * width, width)].astype(jnp.int32)
                low[:, pl.ds(k * width, width)] = low_onehot(every)
                high[:, pl.ds(k * width, width)] = high_onehot(every, groups)
        wait_scatter(recv_sem.at[2 + it], it)
        spend = part[me] + jnp.sum(got[it], axis=0)
        allspend[it, :, lanes(me)] = spend
        share(allspend.at[it], 4 + it)
        lam = jnp.maximum(0.0, lam + eta * (spend - lim_ref[...]))
        wait_all(allspend.at[it], recv_sem.at[4 + it])

        adv_spend = jnp.zeros((3 * groups, LANES), jnp.float32)
        stretch = min(n, 32) * width
        for first in range(0, n * width, stretch):
            at = pl.ds(first, stretch)
            adv_spend = adv_spend + lax.dot_general(
                split3(high[:, at] * allspend[it, :, at]),
                low[:, at],
                (((1,), (1,)), ((), ())),
                preferred_element_type=jnp.float32,
            )
        mu = jnp.maximum(0.0, mu + eta_adv * (sum3(adv_spend) - adv_lim_ref[...]))
        if it < ITERS - 1:
            mu3 = split3(mu)
            for first in range(0, n * width, stretch):
                at = pl.ds(first, stretch)
                lam_all = jnp.maximum(
                    0.0, static[0:1, at] + eta * (allspend[it, :, at] - static[2:3, at])
                )
                price[it + 1, :, at] = lam_all + take(mu3, low[:, at], high[:, at])
    lam_out[...] = lam
    mu_out[...] = mu
    spend_out[...] = spend
    wait_all(price.at[0], send_sem.at[0])
    wait_all(static, send_sem.at[1])
    wait_scatter(send_sem.at[2 + ITERS - 1], ITERS - 1)
    for it in range(ITERS):
        wait_all(allspend.at[it], send_sem.at[4 + it])


def body(
    n,
    n_dev,
    values,
    costs,
    block_ids,
    row_counts,
    adv_map,
    camp_limits,
    adv_limits,
    camp_duals,
    adv_duals,
):
    blocks, rows, width = values.shape
    owned = camp_duals.shape[0]
    total = owned * n
    num_adv = adv_duals.shape[0]
    groups = num_adv // LANES
    eta = owned // width / (4.0 * rows * blocks)
    eta_adv = num_adv * (owned // width) / (4.0 * rows * blocks * total)
    smem = pl.BlockSpec(memory_space=pltpu.SMEM)
    vmem = pl.BlockSpec(memory_space=pltpu.VMEM)
    hbm = pl.BlockSpec(memory_space=pl.ANY)
    lam, mu, spend = pl.pallas_call(
        functools.partial(kernel, n, n_dev, eta, eta_adv),
        out_shape=(
            jax.ShapeDtypeStruct((1, owned), jnp.float32),
            jax.ShapeDtypeStruct((groups, LANES), jnp.float32),
            jax.ShapeDtypeStruct((1, owned), jnp.float32),
        ),
        in_specs=[smem, hbm, hbm] + [vmem] * 6,
        out_specs=(vmem, vmem, vmem),
        scratch_shapes=[
            pltpu.VMEM((blocks, rows, width), jnp.bfloat16),
            pltpu.VMEM((blocks, rows, width), jnp.bfloat16),
            pltpu.VMEM((ITERS, 1, total), jnp.float32),
            pltpu.VMEM((4, total), jnp.float32),
            pltpu.VMEM((LANES, total), jnp.bfloat16),
            pltpu.VMEM((groups, total), jnp.float32),
            pltpu.VMEM((SLAB + 1, SLAB, LANES), jnp.float32),
            pltpu.VMEM((blocks * SUBLANES, width), jnp.float32),
            pltpu.VMEM((blocks, 1, width), jnp.float32),
            pltpu.VMEM((total // width, 1, width), jnp.float32),
            pltpu.VMEM((ITERS, n - 1, 1, width), jnp.float32),
            pltpu.VMEM((ITERS, 1, total), jnp.float32),
            pltpu.SemaphoreType.DMA((2, CHUNKS)),
            pltpu.SemaphoreType.DMA((6,)),
            pltpu.SemaphoreType.DMA((6,)),
        ],
        compiler_params=pltpu.CompilerParams(
            collective_id=0, has_side_effects=True, vmem_limit_bytes=56 * 1024 * 1024
        ),
        cost_estimate=pl.CostEstimate(
            flops=ITERS * 8 * blocks * rows * width,
            bytes_accessed=4 * blocks * rows * width,
            transcendentals=0,
        ),
    )(
        row_counts,
        values,
        costs,
        block_ids.reshape(1, blocks),
        adv_map.reshape(1, owned),
        camp_limits.reshape(1, owned),
        adv_limits.reshape(groups, LANES),
        camp_duals.reshape(1, owned),
        adv_duals.reshape(groups, LANES),
    )
    return lam.reshape(owned), mu.reshape(num_adv), spend.reshape(owned)


def solution(mesh):
    both = P(("imp", "dev"))
    blocked = P(("imp", "dev"), None, None)
    return jax.shard_map(
        functools.partial(body, mesh.size, mesh.shape["dev"]),
        mesh=mesh,
        in_specs=(blocked, blocked, both, both, both, both, P(), both, P()),
        out_specs=(both, P(), both),
        check_vma=False,
    )
```

time: 326 us -> 49.1 us (0.15)
  blocking collectives: 293 us -> 0 us
  Pallas kernels: 0 us -> 44.5 us
  other arithmetic: 25.8 us -> 0 us
    psum x4 -> x0, blocking collectives: 158 us -> none  [the longest x2 83.6 us: body(): adv_spend = lax.psum(adv_part, ('imp', 'dev'))]
    all_gather x2 -> x0, blocking collectives: 135 us -> none  [body(): lax.all_gather(price_own, ('imp', 'dev'), axis=0, tiled=True)]
    pallas_call x0 -> x1, Pallas kernels: none -> 44.5 us  [body(): pl.pallas_call(functools.partial(kernel, n, n_dev, eta, eta_adv), out_sha...]
    reduce_sum x2 -> x0, other arithmetic: 18.2 us -> none  [local_partial(): contrib = jnp.sum(cost_f * x_val, axis=1)]
    scatter-add x2 -> x0, other arithmetic: 4.16 us -> none  [body(): adv_part = jax.ops.segment_sum(spend, adv_map, num_adv)]
    unnamed x14 -> x3, local copies, waits for them, and re-layouts: 0.07 us -> 3.74 us
    gather x2 -> x0, local copies, waits for them, and re-layouts: 3.66 us -> none  [body(): price_own = lam + mu[adv_map]]
where the time goes in v1:
time: 49.1 us; the launch traced here: 48.8 us
  Pallas kernels  44.5 us (91%)
  local copies, waits for them, and re-layouts  3.74 us (8%)
  between operations  0.64 us (1%)
    pallas_call x1, Pallas kernels, body(): pl.pallas_call(functools.partial(kernel, n, n_dev, eta, eta_adv), out_sha...  44.5 us
    unnamed x3, local copies, waits for them, and re-layouts  3.74 us

profile of v1, /device:TPU:0, one launch (start us, length us, event | category | flops | bytes accessed | tf_op | source)
XLA Modules:
  0.0 48.8 jit_solution(17340151292825107603)
XLA Ops:
  0.6 44.5 %shard_map.112 = (f32[1,256]{1,0:T(1,128)}, f32[16,128]{1,0:T(8,128)}, f32[1,256]{1,0:T(1,128)}) custom-call(s32[64]{0:T(128)} %counts_s.1, bf16[64,256,256]{2,1,0:T(8,128)(2,1)} %values.1, bf16[64,256,256]{2,1,0:T(8,128)(2,1)} %costs.1, s32[1,64]{1,0:T(1,128)} %bitcast.17, s32[1,256]{1,0:T(1,128)} %bitcast.12, f32[1,256]{1,0:T(1,128)} %bitcast.13, ...), custom_call_target="tpu_custom_call" | custom-call | flops 67108864 | bytes 16777216 | tf_op jit(solution)/shard_map/pallas_call | solution.py:285
  45.1 1.2 %copy.15 = f32[256]{0:T(256)} copy(f32[256]{0:T(256)} %bitcast.16) | data formatting | bytes 2048
  46.3 1.3 %copy.16 = f32[2048]{0:T(1024)} copy(f32[2048]{0:T(1024)} %bitcast.11) | data formatting | bytes 16384
  47.6 1.2 %copy.17 = f32[256]{0:T(256)} copy(f32[256]{0:T(256)} %bitcast.15) | data formatting | bytes 2048

commit v2 on v1

--- a/solution.py
+++ b/solution.py
@@ -23,6 +23,11 @@
     return jnp.concatenate([one, two, three], axis=0)
 
 
+def split2(x):
+    one = x.astype(jnp.bfloat16)
+    return jnp.concatenate([one, (x - one.astype(jnp.float32)).astype(jnp.bfloat16)], axis=0)
+
+
 def sum3(x):
     m = x.shape[0] // 3
     return x[:m] + x[m : 2 * m] + x[2 * m :]
@@ -51,6 +56,7 @@
     n_dev,
     eta,
     eta_adv,
+    ids_s,
     counts_s,
     values,
     costs,
@@ -60,9 +66,7 @@
     adv_lim_ref,
     lam_ref,
     mu_ref,
-    lam_out,
-    mu_out,
-    spend_out,
+    result,
     vbuf,
     cbuf,
     price,
@@ -71,7 +75,6 @@
     high,
     cap,
     contrib,
-    asked,
     part,
     got,
     allspend,
@@ -111,9 +114,10 @@
         return pl.ds(pl.multiple_of(k * width, width), width)
 
     def share(ref, phase):
+        spot = ref.at[me] if len(ref.shape) == 3 else ref.at[:, lanes(me)]
+
         @pl.loop(1, n)
         def _(d):
-            spot = ref.at[:, lanes(me)]
             pltpu.make_async_remote_copy(
                 src_ref=spot,
                 dst_ref=spot,
@@ -124,7 +128,10 @@
             ).start()
 
     def wait_all(ref, sem):
-        span = ref.at[:, pl.ds(0, (n - 1) * width)]
+        if len(ref.shape) == 3:
+            span = ref.at[pl.ds(0, n - 1)]
+        else:
+            span = ref.at[:, pl.ds(0, (n - 1) * width)]
         pltpu.make_async_copy(span, span, sem).wait()
 
     def scatter(phase):
@@ -147,7 +154,7 @@
     adv = adv_ref[...]
     lam = lam_ref[...]
     mu = mu_ref[...]
-    price[0, :, lanes(me)] = lam + take(split3(mu), low_onehot(adv), high_onehot(adv, groups))
+    price[0, me] = lam + take(split3(mu), low_onehot(adv), high_onehot(adv, groups))
     static[:, lanes(me)] = jnp.concatenate(
         [lam, adv.astype(jnp.float32), lim_ref[...], jnp.zeros_like(lam)], axis=0
     )
@@ -162,18 +169,18 @@
 
     campaign = lax.broadcasted_iota(jnp.int32, (part.shape[0], blocks), 0)
     owner = jnp.where(campaign == ids_v[...], 1.0, 0.0).astype(jnp.bfloat16)
-    asks3 = jnp.concatenate([owner, owner, owner], axis=0)
     wide = lax.broadcasted_iota(jnp.int32, (blocks, blocks * SUBLANES), 1)
     from_block = lax.broadcasted_iota(jnp.int32, (blocks, blocks * SUBLANES), 0)
     spread = jnp.where(lax.shift_right_logical(wide, 3) == from_block, 1.0, 0.0)
     owner = jnp.dot(
         owner, spread.astype(jnp.bfloat16), preferred_element_type=jnp.float32
     ).astype(jnp.bfloat16)
-    owner3 = jnp.concatenate([owner, owner, owner], axis=1)
+    owner2 = jnp.concatenate([owner, owner], axis=1)
 
     def block_pass(b, it):
+        row = price[it, ids_s[b]]
         prices = [
-            jnp.broadcast_to(asked[b, :, h : h + LANES], (SLAB, LANES))
+            jnp.broadcast_to(row[:, h : h + LANES], (SLAB, LANES))
             for h in range(0, width, LANES)
         ]
         totals = [jnp.zeros((SLAB, LANES), jnp.float32) for _ in prices]
@@ -193,14 +200,6 @@
             )
 
     for it in range(ITERS):
-        offers = jnp.concatenate(
-            [price[it, :, pl.ds(k * width, width)] for k in range(part.shape[0])], axis=0
-        )
-        asking = lax.dot_general(
-            asks3, split3(offers), (((0,), (0,)), ((), ())), preferred_element_type=jnp.float32
-        )
-        for b in range(blocks):
-            asked[b] = asking[b : b + 1]
         for i in range(CHUNKS if it == 0 else 1):
             if it == 0:
                 for copy in load(i):
@@ -211,7 +210,7 @@
             def _(b):
                 block_pass(b, it)
 
-        mine = jnp.dot(owner3, split3(contrib[...]), preferred_element_type=jnp.float32)
+        mine = jnp.dot(owner2, split2(contrib[...]), preferred_element_type=jnp.float32)
         if it > 0:
             wait_scatter(send_sem.at[2 + it - 1], it - 1)
         for k in range(part.shape[0]):
@@ -248,15 +247,29 @@
                 lam_all = jnp.maximum(
                     0.0, static[0:1, at] + eta * (allspend[it, :, at] - static[2:3, at])
                 )
-                price[it + 1, :, at] = lam_all + take(mu3, low[:, at], high[:, at])
-    lam_out[...] = lam
-    mu_out[...] = mu
-    spend_out[...] = spend
+                new = lam_all + take(mu3, low[:, at], high[:, at])
+                for k in range(stretch // width):
+                    price[it + 1, first // width + k] = new[:, k * width : (k + 1) * width]
+    tiles = width // LANES
+    for k in range(tiles):
+        at = slice(k * LANES, (k + 1) * LANES)
+        result[k : k + 1] = lam[:, at]
+        result[tiles + k : tiles + k + 1] = spend[:, at]
+    result[SUBLANES:] = mu
     wait_all(price.at[0], send_sem.at[0])
     wait_all(static, send_sem.at[1])
     wait_scatter(send_sem.at[2 + ITERS - 1], ITERS - 1)
     for it in range(ITERS):
         wait_all(allspend.at[it], send_sem.at[4 + it])
+
+
+def deal(result, lam_out, mu_out, spend_out):
+    tiles = lam_out.shape[1] // LANES
+    for k in range(tiles):
+        at = slice(k * LANES, (k + 1) * LANES)
+        lam_out[:, at] = result[k : k + 1]
+        spend_out[:, at] = result[tiles + k : tiles + k + 1]
+    mu_out[...] = result[SUBLANES:]
 
 
 def body(
@@ -282,25 +295,20 @@
     smem = pl.BlockSpec(memory_space=pltpu.SMEM)
     vmem = pl.BlockSpec(memory_space=pltpu.VMEM)
     hbm = pl.BlockSpec(memory_space=pl.ANY)
-    lam, mu, spend = pl.pallas_call(
+    result = pl.pallas_call(
         functools.partial(kernel, n, n_dev, eta, eta_adv),
-        out_shape=(
-            jax.ShapeDtypeStruct((1, owned), jnp.float32),
-            jax.ShapeDtypeStruct((groups, LANES), jnp.float32),
-            jax.ShapeDtypeStruct((1, owned), jnp.float32),
-        ),
-        in_specs=[smem, hbm, hbm] + [vmem] * 6,
-        out_specs=(vmem, vmem, vmem),
+        out_shape=jax.ShapeDtypeStruct((SUBLANES + groups, LANES), jnp.float32),
+        in_specs=[smem, smem, hbm, hbm] + [vmem] * 6,
+        out_specs=vmem,
         scratch_shapes=[
             pltpu.VMEM((blocks, rows, width), jnp.bfloat16),
             pltpu.VMEM((blocks, rows, width), jnp.bfloat16),
-            pltpu.VMEM((ITERS, 1, total), jnp.float32),
+            pltpu.VMEM((ITERS, n, 1, width), jnp.float32),
             pltpu.VMEM((4, total), jnp.float32),
             pltpu.VMEM((LANES, total), jnp.bfloat16),
             pltpu.VMEM((groups, total), jnp.float32),
             pltpu.VMEM((SLAB + 1, SLAB, LANES), jnp.float32),
             pltpu.VMEM((blocks * SUBLANES, width), jnp.float32),
-            pltpu.VMEM((blocks, 1, width), jnp.float32),
             pltpu.VMEM((total // width, 1, width), jnp.float32),
             pltpu.VMEM((ITERS, n - 1, 1, width), jnp.float32),
             pltpu.VMEM((ITERS, 1, total), jnp.float32),
@@ -317,6 +325,7 @@
             transcendentals=0,
         ),
     )(
+        block_ids,
         row_counts,
         values,
         costs,
@@ -327,6 +336,16 @@
         camp_duals.reshape(1, owned),
         adv_duals.reshape(groups, LANES),
     )
+    lam, mu, spend = pl.pallas_call(
+        deal,
+        out_shape=(
+            jax.ShapeDtypeStruct((1, owned), jnp.float32),
+            jax.ShapeDtypeStruct((groups, LANES), jnp.float32),
+            jax.ShapeDtypeStruct((1, owned), jnp.float32),
+        ),
+        in_specs=[vmem],
+        out_specs=(vmem, vmem, vmem),
+    )(result)
     return lam.reshape(owned), mu.reshape(num_adv), spend.reshape(owned)
 
 

time: 49.1 us -> 46.3 us (0.943)
  local copies, waits for them, and re-layouts: 3.74 us -> 0 us
  Pallas kernels: 44.5 us -> 45.4 us
    unnamed x3 -> x0, local copies, waits for them, and re-layouts: 3.74 us -> none
    pallas_call x0 -> x1, Pallas kernels: none -> 1.31 us  [body(): pl.pallas_call(deal, out_shape=(jax.ShapeDtypeStruct((1, owned), jnp.floa...]
where the time goes in v2:
time: 46.3 us; the launch traced here: 46.1 us
  Pallas kernels  45.4 us (98%)
  between operations  0.64 us (1%)
    pallas_call x1, Pallas kernels, body(): pl.pallas_call(functools.partial(kernel, n, n_dev, eta, eta_adv), out_sha...  44.1 us
    pallas_call x1, Pallas kernels, body(): pl.pallas_call(deal, out_shape=(jax.ShapeDtypeStruct((1, owned), jnp.floa...  1.31 us

profile of v2, /device:TPU:0, one launch (start us, length us, event | category | flops | bytes accessed | tf_op | source)
XLA Modules:
  0.0 46.1 jit_solution(16181516158639340362)
XLA Ops:
  0.6 44.1 %shard_map.112.result = f32[24,128]{1,0:T(8,128)} custom-call(s32[64]{0:T(128)} %ids_s.1, s32[64]{0:T(128)} %counts_s.1, bf16[64,256,256]{2,1,0:T(8,128)(2,1)} %values.1, bf16[64,256,256]{2,1,0:T(8,128)(2,1)} %costs.1, s32[1,64]{1,0:T(1,128)} %bitcast.11, s32[1,256]{1,0:T(1,128)} %bitcast.12, f32[1,256]{1,0:T(1,128)} %bitcast.13, f32[16,128]{1,0:T(8,128)} %bitcast.9, ...), custom_call_target="tpu_custom_call" | custom-call | flops 67108864 | bytes 16777216 | tf_op jit(solution)/shard_map/pallas_call | solution.py:298
  44.8 1.3 %shard_map.113 = (f32[1,256]{1,0:T(1,128)}, f32[16,128]{1,0:T(8,128)}, f32[1,256]{1,0:T(1,128)}) custom-call(f32[24,128]{1,0:T(8,128)} %shard_map.112.result), custom_call_target="tpu_custom_call" | custom-call | tf_op jit(solution)/shard_map/pallas_call | solution.py:339

commit v3 on v2

--- a/solution.py
+++ b/solution.py
@@ -11,7 +11,7 @@
 LANES = 128
 SLAB = 16
 SUBLANES = 8
-CHUNKS = 8
+CHUNKS = 4
 MESH = pl.DeviceIdType.MESH
 
 
@@ -106,7 +106,7 @@
     def place(k):
         return (k // n_dev, lax.rem(k, n_dev))
 
-    @pl.loop(1, n)
+    @pl.loop(1, n, unroll=True)
     def _(d):
         pl.semaphore_signal(barrier, inc=1, device_id=place(peer(d)), device_id_type=MESH)
 
@@ -116,7 +116,7 @@
     def share(ref, phase):
         spot = ref.at[me] if len(ref.shape) == 3 else ref.at[:, lanes(me)]
 
-        @pl.loop(1, n)
+        @pl.loop(1, n, unroll=True)
         def _(d):
             pltpu.make_async_remote_copy(
                 src_ref=spot,
@@ -135,7 +135,7 @@
         pltpu.make_async_copy(span, span, sem).wait()
 
     def scatter(phase):
-        @pl.loop(1, n)
+        @pl.loop(1, n, unroll=True)
         def _(d):
             to = peer(d)
             pltpu.make_async_remote_copy(
@@ -206,7 +206,7 @@
                     copy.wait()
             span = step_blocks if it == 0 else blocks
 
-            @pl.loop(i * span, (i + 1) * span)
+            @pl.loop(i * span, (i + 1) * span, unroll=2)
             def _(b):
                 block_pass(b, it)
 

time: 46.3 us -> 44.9 us (0.970)
  Pallas kernels: 45.4 us -> 44 us
    pallas_call x1, Pallas kernels: 44.1 us -> 42.7 us  [body(): pl.pallas_call(functools.partial(kernel, n, n_dev, eta, eta_adv), out_sha...]
where the time goes in v3:
time: 44.9 us; the launch traced here: 44.6 us
  Pallas kernels  44 us (98%)
  between operations  0.64 us (1%)
    pallas_call x1, Pallas kernels, body(): pl.pallas_call(functools.partial(kernel, n, n_dev, eta, eta_adv), out_sha...  42.7 us
    pallas_call x1, Pallas kernels, body(): pl.pallas_call(deal, out_shape=(jax.ShapeDtypeStruct((1, owned), jnp.floa...  1.31 us

profile of v3, /device:TPU:0, one launch (start us, length us, event | category | flops | bytes accessed | tf_op | source)
XLA Modules:
  0.0 44.6 jit_solution(16080232490977098521)
XLA Ops:
  0.6 42.7 %shard_map.112.result = f32[24,128]{1,0:T(8,128)} custom-call(s32[64]{0:T(128)} %ids_s.1, s32[64]{0:T(128)} %counts_s.1, bf16[64,256,256]{2,1,0:T(8,128)(2,1)} %values.1, bf16[64,256,256]{2,1,0:T(8,128)(2,1)} %costs.1, s32[1,64]{1,0:T(1,128)} %bitcast.11, s32[1,256]{1,0:T(1,128)} %bitcast.12, f32[1,256]{1,0:T(1,128)} %bitcast.13, f32[16,128]{1,0:T(8,128)} %bitcast.9, ...), custom_call_target="tpu_custom_call" | custom-call | flops 67108864 | bytes 16777216 | tf_op jit(solution)/shard_map/pallas_call | solution.py:298
  43.3 1.3 %shard_map.113 = (f32[1,256]{1,0:T(1,128)}, f32[16,128]{1,0:T(8,128)}, f32[1,256]{1,0:T(1,128)}) custom-call(f32[24,128]{1,0:T(8,128)} %shard_map.112.result), custom_call_target="tpu_custom_call" | custom-call | tf_op jit(solution)/shard_map/pallas_call | solution.py:339

commit v4 on v3

--- a/solution.py
+++ b/solution.py
@@ -73,6 +73,8 @@
     static,
     low,
     high,
+    vwide,
+    cwide,
     cap,
     contrib,
     part,
@@ -164,8 +166,8 @@
 
     pl.semaphore_wait(barrier, n - 1)
     share(price.at[0], 0)
+    wait_all(price.at[0], recv_sem.at[0])
     share(static, 1)
-    wait_all(price.at[0], recv_sem.at[0])
 
     campaign = lax.broadcasted_iota(jnp.int32, (part.shape[0], blocks), 0)
     owner = jnp.where(campaign == ids_v[...], 1.0, 0.0).astype(jnp.bfloat16)
@@ -177,7 +179,7 @@
     ).astype(jnp.bfloat16)
     owner2 = jnp.concatenate([owner, owner], axis=1)
 
-    def block_pass(b, it):
+    def block_pass(b, it, vfrom, cfrom):
         row = price[it, ids_s[b]]
         prices = [
             jnp.broadcast_to(row[:, h : h + LANES], (SLAB, LANES))
@@ -189,8 +191,8 @@
             top = cap[jnp.minimum(jnp.maximum(count - s, 0), SLAB)]
             for h, p in enumerate(prices):
                 at = pl.ds(h * LANES, LANES)
-                v = vbuf[b, pl.ds(s, SLAB), at].astype(jnp.float32)
-                c = cbuf[b, pl.ds(s, SLAB), at].astype(jnp.float32)
+                v = vfrom[b, pl.ds(s, SLAB), at].astype(jnp.float32)
+                c = cfrom[b, pl.ds(s, SLAB), at].astype(jnp.float32)
                 x = jnp.minimum(jnp.maximum(v - c * p, 0.0), top)
                 totals[h] = totals[h] + c * x
         for h, total in enumerate(totals):
@@ -200,15 +202,17 @@
             )
 
     for it in range(ITERS):
-        for i in range(CHUNKS if it == 0 else 1):
+        for i in range(CHUNKS):
             if it == 0:
                 for copy in load(i):
                     copy.wait()
-            span = step_blocks if it == 0 else blocks
-
-            @pl.loop(i * span, (i + 1) * span, unroll=2)
+            span = step_blocks
+            wide_now = it > 0 and i == 0
+            vfrom, cfrom = (vwide, cwide) if wide_now else (vbuf, cbuf)
+
+            @pl.loop(i * span, (i + 1) * span, unroll=4)
             def _(b):
-                block_pass(b, it)
+                block_pass(b, it, vfrom, cfrom)
 
         mine = jnp.dot(owner2, split2(contrib[...]), preferred_element_type=jnp.float32)
         if it > 0:
@@ -227,6 +231,13 @@
         allspend[it, :, lanes(me)] = spend
         share(allspend.at[it], 4 + it)
         lam = jnp.maximum(0.0, lam + eta * (spend - lim_ref[...]))
+        if it == 0:
+
+            @pl.loop(0, blocks // CHUNKS)
+            def _(b):
+                vwide[b] = vbuf[b].astype(jnp.float32)
+                cwide[b] = cbuf[b].astype(jnp.float32)
+
         wait_all(allspend.at[it], recv_sem.at[4 + it])
 
         adv_spend = jnp.zeros((3 * groups, LANES), jnp.float32)
@@ -307,6 +318,8 @@
             pltpu.VMEM((4, total), jnp.float32),
             pltpu.VMEM((LANES, total), jnp.bfloat16),
             pltpu.VMEM((groups, total), jnp.float32),
+            pltpu.VMEM((blocks // CHUNKS, rows, width), jnp.float32),
+            pltpu.VMEM((blocks // CHUNKS, rows, width), jnp.float32),
             pltpu.VMEM((SLAB + 1, SLAB, LANES), jnp.float32),
             pltpu.VMEM((blocks * SUBLANES, width), jnp.float32),
             pltpu.VMEM((total // width, 1, width), jnp.float32),

time: 44.9 us -> 44.1 us (0.982)
  Pallas kernels: 44 us -> 43.2 us
    pallas_call x1, Pallas kernels: 42.7 us -> 41.9 us  [body(): pl.pallas_call(functools.partial(kernel, n, n_dev, eta, eta_adv), out_sha...]
where the time goes in v4:
time: 44.1 us; the launch traced here: 43.8 us
  Pallas kernels  43.2 us (98%)
  between operations  0.64 us (1%)
    pallas_call x1, Pallas kernels, body(): pl.pallas_call(functools.partial(kernel, n, n_dev, eta, eta_adv), out_sha...  41.9 us
    pallas_call x1, Pallas kernels, body(): pl.pallas_call(deal, out_shape=(jax.ShapeDtypeStruct((1, owned), jnp.floa...  1.31 us

profile of v4, /device:TPU:0, one launch (start us, length us, event | category | flops | bytes accessed | tf_op | source)
XLA Modules:
  0.0 43.8 jit_solution(15710508366232992285)
XLA Ops:
  0.6 41.9 %shard_map.112.result = f32[24,128]{1,0:T(8,128)} custom-call(s32[64]{0:T(128)} %ids_s.1, s32[64]{0:T(128)} %counts_s.1, bf16[64,256,256]{2,1,0:T(8,128)(2,1)} %values.1, bf16[64,256,256]{2,1,0:T(8,128)(2,1)} %costs.1, s32[1,64]{1,0:T(1,128)} %bitcast.11, s32[1,256]{1,0:T(1,128)} %bitcast.12, f32[1,256]{1,0:T(1,128)} %bitcast.13, f32[16,128]{1,0:T(8,128)} %bitcast.9, ...), custom_call_target="tpu_custom_call" | custom-call | flops 67108864 | bytes 16777216 | tf_op jit(solution)/shard_map/pallas_call | solution.py:309
  42.5 1.3 %shard_map.113 = (f32[1,256]{1,0:T(1,128)}, f32[16,128]{1,0:T(8,128)}, f32[1,256]{1,0:T(1,128)}) custom-call(f32[24,128]{1,0:T(8,128)} %shard_map.112.result), custom_call_target="tpu_custom_call" | custom-call | tf_op jit(solution)/shard_map/pallas_call | solution.py:352
